TPU v7x, 32 devices: a whole 2x2x4 slice. The times are simulated.
32 devices in a mesh: grp: 4 (over y, core), seq: 8 (over z, x).
Axes of the slice: x: 2, y: 2, z: 4, core: 2. Of those that a mesh axis runs over, the one named last changes fastest.
Arguments:
- query: bfloat16 [16384, 1024], P(('grp', 'seq')), may hold values from -6 to 6
- key_in: bfloat16 [16384, 1024], P(('grp', 'seq')), may hold values from -6 to 6
- value: bfloat16 [16384, 1024], P(('grp', 'seq')), may hold values from -6 to 6
- gate: bfloat16 [16384, 1024], P(('grp', 'seq')), may hold values from -6 to 6
- gain: float32 [1024], replicated, may hold values from 0.1 to 1.9
Outputs:
- attended: bfloat16 [16384, 1024], P(('grp', 'seq'))
All inputs are finite; a program needn't handle non-finite values.
Results may differ from a plain program's by a relative error of at most 0.0046.
Values sent between devices are 32-bit elements; how exact they have to be, the bound alone decides.
A program may use at most 320 MiB of HBM per device.

v0:
```python
import jax
import jax.numpy as jnp
from jax import lax
from jax.sharding import PartitionSpec as P

HEADS = 8
HEAD_DIM = 128
BLOCK = 256


def prefix(part, axis, combine, identity):
    place = lax.axis_index(axis)
    gathered = lax.all_gather(part, axis)
    state = jnp.zeros_like(part) + jnp.asarray(identity, part.dtype)

    def one(step, state):
        return combine(state, lax.dynamic_index_in_dim(gathered, step, 0, False))

    return lax.fori_loop(0, place, one, state)


def per_device(query, key_in, value, gate, gain):
    rows_here = query.shape[0]
    count = rows_here // BLOCK
    queries = jax.nn.silu(query.astype(jnp.float32)).astype(jnp.bfloat16)
    keys_act = jax.nn.silu(key_in.astype(jnp.float32)).astype(jnp.bfloat16)
    queries = queries.reshape(count, BLOCK, HEADS, HEAD_DIM)
    keys_act = keys_act.reshape(count, BLOCK, HEADS, HEAD_DIM)
    values_in = value.reshape(count, BLOCK, HEADS, HEAD_DIM)
    block_kv = jnp.einsum(
        "bthd,bthe->bhde", keys_act, values_in, preferred_element_type=jnp.float32
    )
    own_total = jnp.sum(block_kv, axis=0)
    nothing = jnp.zeros_like(own_total)
    within = prefix(own_total, "seq", jnp.add, nothing)
    range_total = lax.psum(own_total, "seq")
    before = prefix(range_total, "grp", jnp.add, nothing)
    carried = before + within
    earlier = jnp.cumsum(block_kv, axis=0) - block_kv + carried[None]
    causal = jnp.arange(BLOCK)[:, None] >= jnp.arange(BLOCK)[None, :]
    scores = jnp.einsum("bthd,bshd->bhts", queries, keys_act, preferred_element_type=jnp.float32)
    scores = jnp.where(causal[None, None], scores, 0.0).astype(jnp.bfloat16)
    inner = jnp.einsum("bhts,bshd->bthd", scores, values_in, preferred_element_type=jnp.float32)
    outer = jnp.einsum(
        "bthd,bhde->bthe", queries.astype(jnp.float32), earlier, precision=lax.Precision.HIGHEST
    )
    mixed = (inner + outer).reshape(rows_here, HEADS, HEAD_DIM)
    power = jnp.mean(mixed * mixed, axis=-1, keepdims=True)
    normed = (mixed / jnp.sqrt(power + 1e-05)).reshape(rows_here, HEADS * HEAD_DIM)
    result = normed * gain[None, :] * jax.nn.sigmoid(gate.astype(jnp.float32))
    return result.astype(jnp.bfloat16)


def solution(mesh):
    return jax.shard_map(
        per_device,
        mesh=mesh,
        in_specs=(
            P(("grp", "seq"), None),
            P(("grp", "seq"), None),
            P(("grp", "seq"), None),
            P(("grp", "seq"), None),
            P(),
        ),
        out_specs=P(("grp", "seq"), None),
        check_vma=False,
    )
```

profile of v0, /device:TPU:31, one launch (start us, length us, event | category | flops | bytes accessed | tf_op | source)
XLA Modules:
  0.0 203.7 jit_solution(9049646495736698907)
XLA Ops:
  6.5 0.0 all-gather.6.cloned.1.call-start
  6.5 1.8 fusion.13
  8.3 0.3 copy.36
  8.6 0.7 copy.28
  9.3 1.5 copy.37
  10.8 1.2 fusion.22
  12.0 0.0 all-gather.6.cloned.1.call-update
  12.0 72.0 %all-gather.6.cloned.1.call-done = f32[64,128,128]{2,1,0:T(8,128)} async-done(((f32[8,128,128]{2,1,0:T(8,128)}), f32[64,128,128]{2,1,0:T(8,128)}) %all-gather.6.cloned.1.call-update) | async-done | bytes 4194320 | tf_op jit(solution)/shard_map/all_gather | solution.py:13
  84.0 0.0 all-reduce.2.cloned.1.call-start
  84.0 0.7 all-reduce.2.cloned.1.call-update
  84.7 0.0 all-gather.4.cloned.1.call-start
  84.8 73.0 %all-reduce.2.cloned.1.call-done = f32[1,8,128,128]{3,2,1,0:T(8,128)} async-done(((f32[1,8,128,128]{3,2,1,0:T(8,128)}), f32[1,8,128,128]{3,2,1,0:T(8,128)}) %all-reduce.2.cloned.1.call-update) | async-done | bytes 524304 | tf_op jit(solution)/shard_map/psum | solution.py:36
  157.8 0.0 all-gather.4.cloned.1.call-update
  157.8 1.8 fusion.14
  159.6 1.2 copy.35
  160.9 3.9 %fusion.11 = f32[2,8,256,128]{2,3,1,0:T(8,128)} fusion(bf16[2,256,8,128]{1,3,2,0:T(8,128)(2,1)S(1)} %copy.28, pred[256,256]{1,0:T(8,128)(4,1)S(1)} %iota_compare_fusion, bf16[2,256,8,128]{3,2,1,0:T(8,128)(2,1)S(1)} %bitcast.47, bf16[2,256,8,128]{3,2,1,0:T(8,128)(2,1)} %bitcast.49), kind=kOutput, calls=%fused_computation.21 | convolution fusion | flops 538968064 | bytes 5308416 | tf_op jit(solution)/shard_map/bhts,bshd->bthd/dot_general | solution.py:43
  164.8 8.4 %while.21 = (s32[]{:T(128)}, f32[8,128,128]{2,1,0:T(8,128)S(1)}, s32[]{:T(128)}, f32[8,8,128,128]{3,2,1,0:T(8,128)}, s32[]{:T(128)}, /*index=5*/s32[]{:T(128)}, s32[]{:T(128)}) while((s32[]{:T(128)}, f32[8,128,128]{2,1,0:T(8,128)S(1)}, s32[]{:T(128)}, f32[8,8,128,128]{3,2,1,0:T(8,128)}, s32[]{:T(128)}, /*index=5*/s32[]{:T(128)}, ...), condition=%wide.region_6.7_spmd, body=%wide.region_5.6_spmd.sunk | while | flops 131077 | bytes 1572987 | solution.py:19
  164.8 1.2 bitcast_add_fusion.6
  166.0 1.2 bitcast_add_fusion.6
  167.2 1.2 bitcast_add_fusion.6
  168.4 1.2 bitcast_add_fusion.6
  169.6 1.2 bitcast_add_fusion.6
  170.8 1.2 bitcast_add_fusion.6
  172.1 1.2 bitcast_add_fusion.6
  173.3 11.2 %all-gather.4.cloned.1.call-done = f32[4,8,128,128]{3,2,1,0:T(8,128)} async-done(((f32[1,8,128,128]{3,2,1,0:T(8,128)}), f32[4,8,128,128]{3,2,1,0:T(8,128)}) %all-gather.4.cloned.1.call-update) | async-done | bytes 2097168 | tf_op jit(solution)/shard_map/all_gather | solution.py:13
  184.5 3.6 %while.20 = (s32[]{:T(128)}, f32[8,128,128]{2,1,0:T(8,128)S(1)}, s32[]{:T(128)}, f32[4,8,128,128]{3,2,1,0:T(8,128)}, s32[]{:T(128)}, /*index=5*/s32[]{:T(128)}, s32[]{:T(128)}) while((s32[]{:T(128)}, f32[8,128,128]{2,1,0:T(8,128)S(1)}, s32[]{:T(128)}, f32[4,8,128,128]{3,2,1,0:T(8,128)}, s32[]{:T(128)}, /*index=5*/s32[]{:T(128)}, ...), condition=%wide.region_4.5_spmd, body=%wide.region_3.4_spmd.sunk | while | flops 131077 | bytes 1572987 | solution.py:19
  184.5 1.2 bitcast_add_fusion.5
  185.7 1.2 bitcast_add_fusion.5
  186.9 1.2 bitcast_add_fusion.5
  188.0 0.1 add.60
  188.1 0.0 copy-start.1
  188.1 0.0 copy-start.2
  188.1 0.3 fusion.12
  188.4 0.9 copy-done.1
  189.3 0.7 copy-done.2
  190.0 1.3 multiply_reduce_fusion
  191.3 0.1 copy.33
  191.5 0.0 copy-start.3
  191.5 1.9 copy.32
  193.4 0.0 copy-start
  193.4 0.0 copy-start.4
  193.4 0.6 div.31
  194.0 0.0 copy-done.3
  194.0 1.0 copy-done
  195.0 0.0 copy-done.4
  195.0 2.2 %fusion.10 = bf16[512,1024]{1,0:T(8,128)(2,1)} fusion(f32[64,8,8,128]{3,2,1,0:T(8,128)S(1)} %bitcast.44, f32[64,8,8,128]{3,2,1,0:T(8,128)S(1)} %bitcast.43, bf16[512,1024]{1,0:T(8,128)(2,1)S(1)} %copy-done.3, f32[1024]{0:T(1024)S(1)} %copy-done.4), kind=kLoop, calls=%fused_computation.18 | loop fusion | flops 4194304 | bytes 6295552 | tf_op jit(solution)/shard_map/convert_element_type | solution.py:51
  (4 shorter events, 0.1 us)
Async XLA Ops:
  6.5 77.5 %all-gather.6.cloned.1.call-start = ((), (), s32[]{:S(2)}) async-start(), calls=%async_computation.2 | async-start | bytes 4718592 | tf_op jit(solution)/shard_map/all_gather | solution.py:13
  84.0 73.8 %all-reduce.2.cloned.1.call-start = ((), (), s32[]{:S(2)}) async-start(), calls=%async_computation | async-start | bytes 1048576 | tf_op jit(solution)/shard_map/psum | solution.py:36
  84.7 99.7 %all-gather.4.cloned.1.call-start = ((), (), s32[]{:S(2)}) async-start(), calls=%async_computation.1 | async-start | bytes 2621440 | tf_op jit(solution)/shard_map/all_gather | solution.py:13
  188.1 1.2 copy-start.1
  188.1 1.9 copy-start.2
  191.5 2.5 %copy-start.3 = (bf16[512,1024]{1,0:T(8,128)(2,1)S(1)}, bf16[512,1024]{1,0:T(8,128)(2,1)}, u32[]{:S(2)}) copy-start(bf16[512,1024]{1,0:T(8,128)(2,1)} %param.12) | copy-start | bytes 3145732
  193.4 1.6 copy-start
  193.4 1.6 copy-start.4
Sparse Core Ops, SparseCore 0:
  12.1 71.8 all-gather.5
  88.2 69.4 all-reduce.1
  159.4 24.9 all-gather.3
where the time goes:
time: 205 us; the launch traced here: 204 us
  waiting for transfers between devices  157 us (77%)
  other arithmetic  18 us (9%)
  between operations  13.2 us (6%)
  local copies, waits for them, and re-layouts  8.98 us (4%)
  matrix products  6.4 us (3%)
    all_gather x2, waiting for transfers between devices, prefix(): gathered = lax.all_gather(part, axis)  83.1 us
    psum x1, waiting for transfers between devices, per_device(): range_total = lax.psum(own_total, 'seq')  73 us
    add x10, other arithmetic, one(): return combine(state, lax.dynamic_index_in_dim(gathered, step, 0, False))  11.8 us
    unnamed x13, local copies, waits for them, and re-layouts  5.62 us
  transfers between devices with their start and end apart: 3, of which 3 were waited for; matrix products, arithmetic and copies ran while one was open for 7% of the time, Pallas kernels for 0%

commit v1 on v0

v1 whole, which is shorter than its diff:
```python
import functools

import jax
import jax.numpy as jnp
from jax import lax
from jax.experimental import pallas as pl
from jax.experimental.pallas import tpu as pltpu
from jax.sharding import PartitionSpec as P

HEADS = 8
HEAD_DIM = 128
BLOCK = 256
MESH = pl.DeviceIdType.MESH
F32 = jnp.float32
BF16 = jnp.bfloat16


def silu(u):
    u = u.astype(F32)
    return (u / (1.0 + jnp.exp(-u))).astype(BF16)


def kernel(m, n, q_ref, k_ref, v_ref, gate_ref, gain_ref, out_ref, ks, qs, own, first, gather, bases, total,
           state, inner, send1, recv1, send2, recv2, send3, recv3):
    g = lax.axis_index("grp")
    me = lax.axis_index("seq")
    rows = q_ref.shape[0]
    count = rows // BLOCK
    piece = HEADS * HEAD_DIM // n
    per_head = n // HEADS

    def rows_of(j):
        return pl.ds(pl.multiple_of(j * piece, piece), piece)

    barrier = pltpu.get_barrier_semaphore()

    def greet_seq(d, c):
        pl.semaphore_signal(barrier, inc=1, device_id={"seq": lax.rem(me + d, n)}, device_id_type=MESH)
        return c

    def greet_grp(d, c):
        pl.semaphore_signal(barrier, inc=1, device_id={"grp": lax.rem(g + d, m)}, device_id_type=MESH)
        return c

    lax.fori_loop(1, n, greet_seq, 0)
    lax.fori_loop(1, m, greet_grp, 0)

    def sums(h, c):
        cols = pl.ds(pl.multiple_of(h * HEAD_DIM, HEAD_DIM), HEAD_DIM)
        acc = None
        for b in range(count):
            r = pl.ds(b * BLOCK, BLOCK)
            key = silu(k_ref[r, cols])
            ks[r, cols] = key
            kv = lax.dot_general(key, v_ref[r, cols], (((0,), (0,)), ((), ())), preferred_element_type=F32)
            acc = kv if acc is None else acc + kv
            if b < count - 1:
                first[b, cols, :] = acc
        own[cols, :] = acc
        return c

    lax.fori_loop(0, HEADS, sums, 0)
    pl.semaphore_wait(barrier, n - 1 + m - 1)

    def scatter(j, sender):
        return pltpu.make_async_remote_copy(
            src_ref=own.at[rows_of(j)], dst_ref=gather.at[sender], send_sem=send1.at[j],
            recv_sem=recv1.at[sender], device_id={"seq": j}, device_id_type=MESH)

    def start1(d, c):
        scatter(lax.rem(me + d, n), me).start()
        return c

    lax.fori_loop(1, n, start1, 0)
    gather[me] = own[rows_of(me), :]

    causal = lax.broadcasted_iota(jnp.int32, (BLOCK, BLOCK), 0) >= lax.broadcasted_iota(jnp.int32, (BLOCK, BLOCK), 1)

    def inside(h, c):
        cols = pl.ds(pl.multiple_of(h * HEAD_DIM, HEAD_DIM), HEAD_DIM)
        for b in range(count):
            r = pl.ds(b * BLOCK, BLOCK)
            query = silu(q_ref[r, cols])
            qs[r, cols] = query
            scores = lax.dot_general(query, ks[r, cols], (((1,), (1,)), ((), ())), preferred_element_type=F32)
            scores = jnp.where(causal, scores, 0.0).astype(BF16)
            inner[r, cols] = jnp.dot(scores, v_ref[r, cols], preferred_element_type=F32)
        return c

    lax.fori_loop(0, HEADS, inside, 0)

    def wait1(d, c):
        scatter(me, lax.rem(me + d, n)).wait_recv()
        return c

    lax.fori_loop(1, n, wait1, 0)
    total[...] = lax.fori_loop(1, n, lambda s, t: t + gather[s], gather[0])

    def share(j, sender):
        return pltpu.make_async_remote_copy(
            src_ref=total, dst_ref=bases.at[sender], send_sem=send2.at[j],
            recv_sem=recv2.at[sender], device_id={"grp": j}, device_id_type=MESH)

    def start2(j, c):
        share(j, g).start()
        return c

    lax.fori_loop(g + 1, m, start2, 0)

    def wait2(j, t):
        share(g, j).wait_recv()
        return t + bases[j]

    base = lax.fori_loop(0, g, wait2, jnp.zeros((piece, HEAD_DIM), F32))

    def running(s, t):
        mine = gather[s]
        gather[s] = t
        return t + mine

    lax.fori_loop(0, n, running, base)

    def spread(j, sender):
        return pltpu.make_async_remote_copy(
            src_ref=gather.at[j], dst_ref=state.at[rows_of(sender)], send_sem=send3.at[j],
            recv_sem=recv3.at[sender], device_id={"seq": j}, device_id_type=MESH)

    def start3(d, c):
        j = lax.rem(me + d, n)
        spread(j, me).start()
        return c

    lax.fori_loop(1, n, start3, 0)
    state[rows_of(me), :] = gather[me]

    def finish(i, c):
        h = lax.rem(me // per_head + HEADS - i, HEADS)
        cols = pl.ds(pl.multiple_of(h * HEAD_DIM, HEAD_DIM), HEAD_DIM)

        def arrive(p, c):
            s = h * per_head + p

            @pl.when(s != me)
            def _():
                spread(me, s).wait_recv()
            return c

        lax.fori_loop(0, per_head, arrive, 0)
        before = state[cols, :]
        for b in range(count):
            r = pl.ds(b * BLOCK, BLOCK)
            now = before if b == 0 else before + first[b - 1, cols, :]
            high = now.astype(BF16)
            low = (now - high.astype(F32)).astype(BF16)
            query = qs[r, cols]
            mixed = inner[r, cols] + jnp.dot(
                jnp.concatenate([query, query], axis=1), jnp.concatenate([high, low], axis=0),
                preferred_element_type=F32)
            power = jnp.mean(mixed * mixed, axis=-1, keepdims=True)
            scale = gain_ref[0:1, cols] / (1.0 + jnp.exp(-gate_ref[r, cols].astype(F32)))
            out_ref[r, cols] = (mixed * lax.rsqrt(power + 1e-05) * scale).astype(BF16)
        return c

    lax.fori_loop(0, HEADS, finish, 0)

    def sent(d, c):
        j = lax.rem(me + d, n)
        scatter(j, me).wait_send()
        spread(j, me).wait_send()
        return c

    lax.fori_loop(1, n, sent, 0)

    def sent2(j, c):
        share(j, g).wait_send()
        return c

    lax.fori_loop(g + 1, m, sent2, 0)


def per_device(m, n, query, key_in, value, gate, gain):
    rows, features = query.shape
    count = rows // BLOCK
    piece = features // n
    whole = pl.BlockSpec(memory_space=pltpu.VMEM)
    dma = pltpu.SemaphoreType.DMA
    return pl.pallas_call(
        functools.partial(kernel, m, n),
        out_shape=jax.ShapeDtypeStruct((rows, features), BF16),
        in_specs=[whole] * 5,
        out_specs=whole,
        scratch_shapes=[
            pltpu.VMEM((rows, features), BF16),
            pltpu.VMEM((rows, features), BF16),
            pltpu.VMEM((features, HEAD_DIM), F32),
            pltpu.VMEM((max(count - 1, 1), features, HEAD_DIM), F32),
            pltpu.VMEM((n, piece, HEAD_DIM), F32),
            pltpu.VMEM((m, piece, HEAD_DIM), F32),
            pltpu.VMEM((piece, HEAD_DIM), F32),
            pltpu.VMEM((features, HEAD_DIM), F32),
            pltpu.VMEM((rows, features), F32),
            dma((n,)), dma((n,)), dma((m,)), dma((m,)), dma((n,)), dma((n,)),
        ],
        compiler_params=pltpu.CompilerParams(
            collective_id=0, has_side_effects=True, vmem_limit_bytes=40 * 1024 * 1024),
    )(query, key_in, value, gate, gain.reshape(1, features))


def solution(mesh):
    m, n = mesh.shape["grp"], mesh.shape["seq"]
    return jax.shard_map(
        functools.partial(per_device, m, n),
        mesh=mesh,
        in_specs=(
            P(("grp", "seq"), None),
            P(("grp", "seq"), None),
            P(("grp", "seq"), None),
            P(("grp", "seq"), None),
            P(),
        ),
        out_specs=P(("grp", "seq"), None),
        check_vma=False,
    )
```

time: 205 us -> 40.7 us (0.20)
  waiting for transfers between devices: 157 us -> 0 us
  Pallas kernels: 0 us -> 33.9 us
  other arithmetic: 18 us -> 0 us
  between operations: 13.2 us -> 0.01 us
  matrix products: 6.4 us -> 0 us
  local copies, waits for them, and re-layouts: 8.98 us -> 6.56 us
    all_gather x2 -> x0, waiting for transfers between devices: 83.1 us -> none  [prefix(): gathered = lax.all_gather(part, axis)]
    psum x1 -> x0, waiting for transfers between devices: 73 us -> none  [per_device(): range_total = lax.psum(own_total, 'seq')]
    pallas_call x0 -> x1, Pallas kernels: none -> 33.9 us  [per_device(): pl.pallas_call(functools.partial(kernel, m, n), out_shape=jax.ShapeDtypeS...]
    add x11 -> x0, other arithmetic: 11.9 us -> none  [the longest x10 11.8 us: one(): return combine(state, lax.dynamic_index_in_dim(gathered, step, 0, False))]
    dot_general x3 -> x0, matrix products: 6.4 us -> none  [the longest x1 3.89 us: per_device(): jnp.einsum('bhts,bshd->bthd', scores, values_in, preferred_element_type=j...]
    unnamed x2 -> x0, other arithmetic: 3.55 us -> none
    convert_element_type x1 -> x0, other arithmetic: 2.23 us -> none  [per_device(): return result.astype(jnp.bfloat16)]
    unnamed x13 -> x11, local copies, waits for them, and re-layouts: 5.62 us -> 6.56 us
  transfers between devices with their start and end apart: 3 -> 0, of which waited for: 3 -> 0; matrix products, arithmetic and copies ran while one was open for 7% -> 0% of each run, Pallas kernels for 0% -> 0%
where the time goes in v1:
time: 40.7 us; the launch traced here: 40.4 us
  Pallas kernels  33.9 us (83%)
  local copies, waits for them, and re-layouts  6.56 us (16%)
    pallas_call x1, Pallas kernels, per_device(): pl.pallas_call(functools.partial(kernel, m, n), out_shape=jax.ShapeDtypeS...  33.9 us
    unnamed x11, local copies, waits for them, and re-layouts  6.56 us

profile of v1, /device:TPU:31, one launch (start us, length us, event | category | flops | bytes accessed | tf_op | source)
XLA Modules:
  0.0 40.4 jit_solution(10791333694012521131)
XLA Ops:
  0.0 0.0 copy-start
  0.0 1.2 %copy-done = bf16[512,1024]{1,0:T(8,128)(2,1)S(1)} copy-done((bf16[512,1024]{1,0:T(8,128)(2,1)S(1)}, bf16[512,1024]{1,0:T(8,128)(2,1)}, u32[]{:S(2)}) %copy-start) | copy-done | bytes 1048600
  1.2 0.0 copy-start.1
  1.2 1.2 %copy-done.1 = bf16[512,1024]{1,0:T(8,128)(2,1)S(1)} copy-done((bf16[512,1024]{1,0:T(8,128)(2,1)S(1)}, bf16[512,1024]{1,0:T(8,128)(2,1)}, u32[]{:S(2)}) %copy-start.1) | copy-done | bytes 1048600
  2.5 0.0 copy-start.2
  2.5 1.2 %copy-done.2 = bf16[512,1024]{1,0:T(8,128)(2,1)S(1)} copy-done((bf16[512,1024]{1,0:T(8,128)(2,1)S(1)}, bf16[512,1024]{1,0:T(8,128)(2,1)}, u32[]{:S(2)}) %copy-start.2) | copy-done | bytes 1048600
  3.7 0.0 copy-start.3
  3.7 1.2 %copy-done.3 = bf16[512,1024]{1,0:T(8,128)(2,1)S(1)} copy-done((bf16[512,1024]{1,0:T(8,128)(2,1)S(1)}, bf16[512,1024]{1,0:T(8,128)(2,1)}, u32[]{:S(2)}) %copy-start.3) | copy-done | bytes 1048600
  4.9 0.0 copy-start.4
  4.9 0.7 %copy-done.4 = f32[1024]{0:T(1024)S(1)} copy-done((f32[1024]{0:T(1024)S(1)}, f32[1024]{0:T(1024)}, u32[]{:S(2)}) %copy-start.4) | copy-done | bytes 4120
  5.6 33.9 %shard_map.55 = bf16[512,1024]{1,0:T(8,128)(2,1)S(1)} custom-call(bf16[512,1024]{1,0:T(8,128)(2,1)S(1)} %copy-done, bf16[512,1024]{1,0:T(8,128)(2,1)S(1)} %copy-done.1, bf16[512,1024]{1,0:T(8,128)(2,1)S(1)} %copy-done.2, bf16[512,1024]{1,0:T(8,128)(2,1)S(1)} %copy-done.3, f32[1,1024]{1,0:T(1,128)S(1)} %bitcast.1), custom_call_target="tpu_custom_call" | custom-call | tf_op jit(solution)/shard_map/pallas_call | solution.py:187
  39.5 1.0 %copy.7 = bf16[512,1024]{1,0:T(8,128)(2,1)} copy(bf16[512,1024]{1,0:T(8,128)(2,1)S(1)} %shard_map.55) | data formatting | bytes 2097152
Async XLA Ops:
  0.0 1.2 %copy-start = (bf16[512,1024]{1,0:T(8,128)(2,1)S(1)}, bf16[512,1024]{1,0:T(8,128)(2,1)}, u32[]{:S(2)}) copy-start(bf16[512,1024]{1,0:T(8,128)(2,1)} %q_ref.1) | copy-start | bytes 3145732
  1.2 1.2 %copy-start.1 = (bf16[512,1024]{1,0:T(8,128)(2,1)S(1)}, bf16[512,1024]{1,0:T(8,128)(2,1)}, u32[]{:S(2)}) copy-start(bf16[512,1024]{1,0:T(8,128)(2,1)} %k_ref.1) | copy-start | bytes 3145732
  2.5 1.2 %copy-start.2 = (bf16[512,1024]{1,0:T(8,128)(2,1)S(1)}, bf16[512,1024]{1,0:T(8,128)(2,1)}, u32[]{:S(2)}) copy-start(bf16[512,1024]{1,0:T(8,128)(2,1)} %v_ref.1) | copy-start | bytes 3145732
  3.7 1.2 %copy-start.3 = (bf16[512,1024]{1,0:T(8,128)(2,1)S(1)}, bf16[512,1024]{1,0:T(8,128)(2,1)}, u32[]{:S(2)}) copy-start(bf16[512,1024]{1,0:T(8,128)(2,1)} %gate_ref.1) | copy-start | bytes 3145732
  4.9 0.7 %copy-start.4 = (f32[1024]{0:T(1024)S(1)}, f32[1024]{0:T(1024)}, u32[]{:S(2)}) copy-start(f32[1024]{0:T(1024)} %param.9) | copy-start | bytes 12292

commit v2 on v1

--- a/solution.py
+++ b/solution.py
@@ -20,8 +20,8 @@
     return (u / (1.0 + jnp.exp(-u))).astype(BF16)
 
 
-def kernel(m, n, q_ref, k_ref, v_ref, gate_ref, gain_ref, out_ref, ks, qs, own, first, gather, bases, total,
-           state, inner, send1, recv1, send2, recv2, send3, recv3):
+def kernel(m, n, q_hbm, k_hbm, v_hbm, gate_hbm, gain_ref, out_hbm, out_ref, q_ref, k_ref, v_ref, gate_ref, scale, ks, qs, own, first, gather, bases, total,
+           state, inner, send1, recv1, send2, recv2, send3, recv3, k_sem, v_sem, q_sem, gate_sem, out_sem):
     g = lax.axis_index("grp")
     me = lax.axis_index("seq")
     rows = q_ref.shape[0]
@@ -45,8 +45,35 @@
     lax.fori_loop(1, n, greet_seq, 0)
     lax.fori_loop(1, m, greet_grp, 0)
 
-    def sums(h, c):
-        cols = pl.ds(pl.multiple_of(h * HEAD_DIM, HEAD_DIM), HEAD_DIM)
+    def turn(i):
+        return lax.rem(me // per_head + 1 + i, HEADS)
+
+    def load(src, dst, sem, h):
+        cols = pl.ds(pl.multiple_of(h * HEAD_DIM, HEAD_DIM), HEAD_DIM)
+        return pltpu.make_async_copy(src.at[:, cols], dst.at[:, cols], sem.at[h])
+
+    def loads(i, c):
+        load(k_hbm, k_ref, k_sem, turn(i)).start()
+        load(v_hbm, v_ref, v_sem, turn(i)).start()
+        return c
+
+    lax.fori_loop(0, HEADS, loads, 0)
+    load_q = pltpu.make_async_copy(q_hbm, q_ref, q_sem)
+    load_gate = pltpu.make_async_copy(gate_hbm, gate_ref, gate_sem)
+    load_q.start()
+    load_gate.start()
+    pl.semaphore_wait(barrier, n - 1 + m - 1)
+
+    def scatter(j, sender):
+        return pltpu.make_async_remote_copy(
+            src_ref=own.at[rows_of(j)], dst_ref=gather.at[sender], send_sem=send1.at[j],
+            recv_sem=recv1.at[sender], device_id={"seq": j}, device_id_type=MESH)
+
+    def sums(i, c):
+        h = turn(i)
+        cols = pl.ds(pl.multiple_of(h * HEAD_DIM, HEAD_DIM), HEAD_DIM)
+        load(k_hbm, k_ref, k_sem, h).wait()
+        load(v_hbm, v_ref, v_sem, h).wait()
         acc = None
         for b in range(count):
             r = pl.ds(b * BLOCK, BLOCK)
@@ -57,21 +84,19 @@
             if b < count - 1:
                 first[b, cols, :] = acc
         own[cols, :] = acc
+
+        def send(p, c):
+            j = h * per_head + p
+
+            @pl.when(j != me)
+            def _():
+                scatter(j, me).start()
+            return c
+
+        lax.fori_loop(0, per_head, send, 0)
         return c
 
     lax.fori_loop(0, HEADS, sums, 0)
-    pl.semaphore_wait(barrier, n - 1 + m - 1)
-
-    def scatter(j, sender):
-        return pltpu.make_async_remote_copy(
-            src_ref=own.at[rows_of(j)], dst_ref=gather.at[sender], send_sem=send1.at[j],
-            recv_sem=recv1.at[sender], device_id={"seq": j}, device_id_type=MESH)
-
-    def start1(d, c):
-        scatter(lax.rem(me + d, n), me).start()
-        return c
-
-    lax.fori_loop(1, n, start1, 0)
     gather[me] = own[rows_of(me), :]
 
     causal = lax.broadcasted_iota(jnp.int32, (BLOCK, BLOCK), 0) >= lax.broadcasted_iota(jnp.int32, (BLOCK, BLOCK), 1)
@@ -85,8 +110,11 @@
             scores = lax.dot_general(query, ks[r, cols], (((1,), (1,)), ((), ())), preferred_element_type=F32)
             scores = jnp.where(causal, scores, 0.0).astype(BF16)
             inner[r, cols] = jnp.dot(scores, v_ref[r, cols], preferred_element_type=F32)
-        return c
-
+            scale[r, cols] = gain_ref[0:1, cols] / (1.0 + jnp.exp(-gate_ref[r, cols].astype(F32)))
+        return c
+
+    load_q.wait()
+    load_gate.wait()
     lax.fori_loop(0, HEADS, inside, 0)
 
     def wait1(d, c):
@@ -157,11 +185,17 @@
                 jnp.concatenate([query, query], axis=1), jnp.concatenate([high, low], axis=0),
                 preferred_element_type=F32)
             power = jnp.mean(mixed * mixed, axis=-1, keepdims=True)
-            scale = gain_ref[0:1, cols] / (1.0 + jnp.exp(-gate_ref[r, cols].astype(F32)))
-            out_ref[r, cols] = (mixed * lax.rsqrt(power + 1e-05) * scale).astype(BF16)
+            out_ref[r, cols] = (mixed * lax.rsqrt(power + 1e-05) * scale[r, cols]).astype(BF16)
+        load(out_ref, out_hbm, out_sem, h).start()
         return c
 
     lax.fori_loop(0, HEADS, finish, 0)
+
+    def stored(h, c):
+        load(out_ref, out_hbm, out_sem, h).wait()
+        return c
+
+    lax.fori_loop(0, HEADS, stored, 0)
 
     def sent(d, c):
         j = lax.rem(me + d, n)
@@ -187,9 +221,15 @@
     return pl.pallas_call(
         functools.partial(kernel, m, n),
         out_shape=jax.ShapeDtypeStruct((rows, features), BF16),
-        in_specs=[whole] * 5,
-        out_specs=whole,
+        in_specs=[pl.BlockSpec(memory_space=pltpu.HBM)] * 4 + [whole],
+        out_specs=pl.BlockSpec(memory_space=pltpu.HBM),
         scratch_shapes=[
+            pltpu.VMEM((rows, features), BF16),
+            pltpu.VMEM((rows, features), BF16),
+            pltpu.VMEM((rows, features), BF16),
+            pltpu.VMEM((rows, features), BF16),
+            pltpu.VMEM((rows, features), BF16),
+            pltpu.VMEM((rows, features), F32),
             pltpu.VMEM((rows, features), BF16),
             pltpu.VMEM((rows, features), BF16),
             pltpu.VMEM((features, HEAD_DIM), F32),
@@ -200,9 +240,10 @@
             pltpu.VMEM((features, HEAD_DIM), F32),
             pltpu.VMEM((rows, features), F32),
             dma((n,)), dma((n,)), dma((m,)), dma((m,)), dma((n,)), dma((n,)),
+            dma((HEADS,)), dma((HEADS,)), dma, dma, dma((HEADS,)),
         ],
         compiler_params=pltpu.CompilerParams(
-            collective_id=0, has_side_effects=True, vmem_limit_bytes=40 * 1024 * 1024),
+            collective_id=0, has_side_effects=True, vmem_limit_bytes=62 * 1024 * 1024),
     )(query, key_in, value, gate, gain.reshape(1, features))
 
 

time: 40.7 us -> 39.4 us (0.968)
  local copies, waits for them, and re-layouts: 6.56 us -> 2.26 us
  Pallas kernels: 33.9 us -> 37 us
    unnamed x11 -> x1, local copies, waits for them, and re-layouts: 6.56 us -> 2.26 us
    pallas_call x1, Pallas kernels: 33.9 us -> 37 us  [per_device(): pl.pallas_call(functools.partial(kernel, m, n), out_shape=jax.ShapeDtypeS...]
where the time goes in v2:
time: 39.4 us; the launch traced here: 39.3 us
  Pallas kernels  37 us (94%)
  local copies, waits for them, and re-layouts  2.26 us (6%)
    pallas_call x1, Pallas kernels, per_device(): pl.pallas_call(functools.partial(kernel, m, n), out_shape=jax.ShapeDtypeS...  37 us
    unnamed x1, local copies, waits for them, and re-layouts  2.26 us

profile of v2, /device:TPU:31, one launch (start us, length us, event | category | flops | bytes accessed | tf_op | source)
XLA Modules:
  0.0 39.3 jit_solution(18126051855168230283)
XLA Ops:
  0.0 37.0 %shard_map.55 = bf16[512,1024]{1,0:T(8,128)(2,1)} custom-call(bf16[512,1024]{1,0:T(8,128)(2,1)} %q_hbm.1, bf16[512,1024]{1,0:T(8,128)(2,1)} %k_hbm.1, bf16[512,1024]{1,0:T(8,128)(2,1)} %v_hbm.1, bf16[512,1024]{1,0:T(8,128)(2,1)} %gate_hbm.1, f32[1,1024]{1,0:T(1,128)} %bitcast.1), custom_call_target="tpu_custom_call" | custom-call | tf_op jit(solution)/shard_map/pallas_call | solution.py:221
  37.0 2.3 %copy.7 = bf16[512,1024]{1,0:T(8,128)(2,1)} copy(bf16[512,1024]{1,0:T(8,128)(2,1)} %shard_map.55) | data formatting | bytes 2097152

commit v3 on v2

--- a/solution.py
+++ b/solution.py
@@ -29,8 +29,13 @@
     piece = HEADS * HEAD_DIM // n
     per_head = n // HEADS
 
+    half = piece // 2
+
     def rows_of(j):
         return pl.ds(pl.multiple_of(j * piece, piece), piece)
+
+    def half_of(j, part):
+        return pl.ds(pl.multiple_of(j * piece + part * half, half), half)
 
     barrier = pltpu.get_barrier_semaphore()
 
@@ -64,10 +69,10 @@
     load_gate.start()
     pl.semaphore_wait(barrier, n - 1 + m - 1)
 
-    def scatter(j, sender):
+    def scatter(j, sender, part):
         return pltpu.make_async_remote_copy(
-            src_ref=own.at[rows_of(j)], dst_ref=gather.at[sender], send_sem=send1.at[j],
-            recv_sem=recv1.at[sender], device_id={"seq": j}, device_id_type=MESH)
+            src_ref=own.at[half_of(j, part)], dst_ref=gather.at[sender, half_of(0, part)],
+            send_sem=send1.at[part, j], recv_sem=recv1.at[part, sender], device_id={"seq": j}, device_id_type=MESH)
 
     def sums(i, c):
         h = turn(i)
@@ -90,13 +95,19 @@
 
             @pl.when(j != me)
             def _():
-                scatter(j, me).start()
+                scatter(j, me, 0).start()
             return c
 
         lax.fori_loop(0, per_head, send, 0)
         return c
 
     lax.fori_loop(0, HEADS, sums, 0)
+
+    def start1(d, c):
+        scatter(lax.rem(me + d, n), me, 1).start()
+        return c
+
+    lax.fori_loop(1, n, start1, 0)
     gather[me] = own[rows_of(me), :]
 
     causal = lax.broadcasted_iota(jnp.int32, (BLOCK, BLOCK), 0) >= lax.broadcasted_iota(jnp.int32, (BLOCK, BLOCK), 1)
@@ -117,48 +128,54 @@
     load_gate.wait()
     lax.fori_loop(0, HEADS, inside, 0)
 
-    def wait1(d, c):
-        scatter(me, lax.rem(me + d, n)).wait_recv()
-        return c
-
-    lax.fori_loop(1, n, wait1, 0)
-    total[...] = lax.fori_loop(1, n, lambda s, t: t + gather[s], gather[0])
-
-    def share(j, sender):
+    def share(j, sender, part):
         return pltpu.make_async_remote_copy(
-            src_ref=total, dst_ref=bases.at[sender], send_sem=send2.at[j],
-            recv_sem=recv2.at[sender], device_id={"grp": j}, device_id_type=MESH)
-
-    def start2(j, c):
-        share(j, g).start()
-        return c
-
-    lax.fori_loop(g + 1, m, start2, 0)
-
-    def wait2(j, t):
-        share(g, j).wait_recv()
-        return t + bases[j]
-
-    base = lax.fori_loop(0, g, wait2, jnp.zeros((piece, HEAD_DIM), F32))
-
-    def running(s, t):
-        mine = gather[s]
-        gather[s] = t
-        return t + mine
-
-    lax.fori_loop(0, n, running, base)
-
-    def spread(j, sender):
+            src_ref=total.at[half_of(0, part)], dst_ref=bases.at[sender, half_of(0, part)],
+            send_sem=send2.at[part, j], recv_sem=recv2.at[part, sender], device_id={"grp": j}, device_id_type=MESH)
+
+    def spread(j, sender, part):
         return pltpu.make_async_remote_copy(
-            src_ref=gather.at[j], dst_ref=state.at[rows_of(sender)], send_sem=send3.at[j],
-            recv_sem=recv3.at[sender], device_id={"seq": j}, device_id_type=MESH)
-
-    def start3(d, c):
-        j = lax.rem(me + d, n)
-        spread(j, me).start()
-        return c
-
-    lax.fori_loop(1, n, start3, 0)
+            src_ref=gather.at[j, half_of(0, part)], dst_ref=state.at[half_of(sender, part)],
+            send_sem=send3.at[part, j], recv_sem=recv3.at[part, sender], device_id={"seq": j}, device_id_type=MESH)
+
+    for part in range(2):
+        here = half_of(0, part)
+
+        def wait1(d, c):
+            scatter(me, lax.rem(me + d, n), part).wait_recv()
+            return c
+
+        lax.fori_loop(1, n, wait1, 0)
+        total[here, :] = lax.fori_loop(1, n, lambda s, t: t + gather[s, here, :], gather[0, here, :])
+
+        def start2(j, c):
+            share(j, g, part).start()
+            return c
+
+        lax.fori_loop(g + 1, m, start2, 0)
+
+    for part in range(2):
+        here = half_of(0, part)
+
+        def wait2(j, t):
+            share(g, j, part).wait_recv()
+            return t + bases[j, here, :]
+
+        base = lax.fori_loop(0, g, wait2, jnp.zeros((half, HEAD_DIM), F32))
+
+        def running(s, t):
+            mine = gather[s, here, :]
+            gather[s, here, :] = t
+            return t + mine
+
+        lax.fori_loop(0, n, running, base)
+
+        def start3(d, c):
+            spread(lax.rem(me + d, n), me, part).start()
+            return c
+
+        lax.fori_loop(1, n, start3, 0)
+
     state[rows_of(me), :] = gather[me]
 
     def finish(i, c):
@@ -170,7 +187,8 @@
 
             @pl.when(s != me)
             def _():
-                spread(me, s).wait_recv()
+                spread(me, s, 0).wait_recv()
+                spread(me, s, 1).wait_recv()
             return c
 
         lax.fori_loop(0, per_head, arrive, 0)
@@ -199,14 +217,16 @@
 
     def sent(d, c):
         j = lax.rem(me + d, n)
-        scatter(j, me).wait_send()
-        spread(j, me).wait_send()
+        for part in range(2):
+            scatter(j, me, part).wait_send()
+            spread(j, me, part).wait_send()
         return c
 
     lax.fori_loop(1, n, sent, 0)
 
     def sent2(j, c):
-        share(j, g).wait_send()
+        share(j, g, 0).wait_send()
+        share(j, g, 1).wait_send()
         return c
 
     lax.fori_loop(g + 1, m, sent2, 0)
@@ -239,7 +259,7 @@
             pltpu.VMEM((piece, HEAD_DIM), F32),
             pltpu.VMEM((features, HEAD_DIM), F32),
             pltpu.VMEM((rows, features), F32),
-            dma((n,)), dma((n,)), dma((m,)), dma((m,)), dma((n,)), dma((n,)),
+            dma((2, n)), dma((2, n)), dma((2, m)), dma((2, m)), dma((2, n)), dma((2, n)),
             dma((HEADS,)), dma((HEADS,)), dma, dma, dma((HEADS,)),
         ],
         compiler_params=pltpu.CompilerParams(

time: 39.4 us -> 37.4 us (0.949)
  the two profiles are of different devices: /device:TPU:31 before, /device:TPU:0 now
where the time goes in v3:
time: 37.4 us; the launch traced here: 37.2 us
  Pallas kernels  35 us (94%)
  local copies, waits for them, and re-layouts  2.26 us (6%)
    pallas_call x1, Pallas kernels, per_device(): pl.pallas_call(functools.partial(kernel, m, n), out_shape=jax.ShapeDtypeS...  35 us
    unnamed x1, local copies, waits for them, and re-layouts  2.26 us

profile of v3, /device:TPU:0, one launch (start us, length us, event | category | flops | bytes accessed | tf_op | source)
XLA Modules:
  0.0 37.2 jit_solution(5571731835824625095)
XLA Ops:
  0.0 35.0 %shard_map.55 = bf16[512,1024]{1,0:T(8,128)(2,1)} custom-call(bf16[512,1024]{1,0:T(8,128)(2,1)} %q_hbm.1, bf16[512,1024]{1,0:T(8,128)(2,1)} %k_hbm.1, bf16[512,1024]{1,0:T(8,128)(2,1)} %v_hbm.1, bf16[512,1024]{1,0:T(8,128)(2,1)} %gate_hbm.1, f32[1,1024]{1,0:T(1,128)} %bitcast.1), custom_call_target="tpu_custom_call" | custom-call | tf_op jit(solution)/shard_map/pallas_call | solution.py:241
  35.0 2.3 %copy.7 = bf16[512,1024]{1,0:T(8,128)(2,1)} copy(bf16[512,1024]{1,0:T(8,128)(2,1)} %shard_map.55) | data formatting | bytes 2097152

commit v4 on v3

--- a/solution.py
+++ b/solution.py
@@ -67,7 +67,6 @@
     load_gate = pltpu.make_async_copy(gate_hbm, gate_ref, gate_sem)
     load_q.start()
     load_gate.start()
-    pl.semaphore_wait(barrier, n - 1 + m - 1)
 
     def scatter(j, sender, part):
         return pltpu.make_async_remote_copy(
@@ -89,6 +88,10 @@
             if b < count - 1:
                 first[b, cols, :] = acc
         own[cols, :] = acc
+        return c
+
+    def post(i, c):
+        h = turn(i)
 
         def send(p, c):
             j = h * per_head + p
@@ -101,7 +104,10 @@
         lax.fori_loop(0, per_head, send, 0)
         return c
 
-    lax.fori_loop(0, HEADS, sums, 0)
+    sums(0, 0)
+    pl.semaphore_wait(barrier, n - 1 + m - 1)
+    post(0, 0)
+    lax.fori_loop(1, HEADS, lambda i, c: post(i, sums(i, c)), 0)
 
     def start1(d, c):
         scatter(lax.rem(me + d, n), me, 1).start()

time: 37.4 us -> 37.1 us (level)
  no operation moved by 1% of the time
where the time goes in v4:
time: 37.1 us; the launch traced here: 36.9 us
  Pallas kernels  34.7 us (94%)
  local copies, waits for them, and re-layouts  2.26 us (6%)
    pallas_call x1, Pallas kernels, per_device(): pl.pallas_call(functools.partial(kernel, m, n), out_shape=jax.ShapeDtypeS...  34.7 us
    unnamed x1, local copies, waits for them, and re-layouts  2.26 us

profile of v4, /device:TPU:0, one launch (start us, length us, event | category | flops | bytes accessed | tf_op | source)
XLA Modules:
  0.0 36.9 jit_solution(14404638832117709848)
XLA Ops:
  0.0 34.7 %shard_map.55 = bf16[512,1024]{1,0:T(8,128)(2,1)} custom-call(bf16[512,1024]{1,0:T(8,128)(2,1)} %q_hbm.1, bf16[512,1024]{1,0:T(8,128)(2,1)} %k_hbm.1, bf16[512,1024]{1,0:T(8,128)(2,1)} %v_hbm.1, bf16[512,1024]{1,0:T(8,128)(2,1)} %gate_hbm.1, f32[1,1024]{1,0:T(1,128)} %bitcast.1), custom_call_target="tpu_custom_call" | custom-call | tf_op jit(solution)/shard_map/pallas_call | solution.py:247
  34.7 2.3 %copy.7 = bf16[512,1024]{1,0:T(8,128)(2,1)} copy(bf16[512,1024]{1,0:T(8,128)(2,1)} %shard_map.55) | data formatting | bytes 2097152
